TPU v7x, 128 devices: a whole 4x4x4 slice. The times are simulated.
128 devices in a mesh: section: 4 (over x_hi, core), seq: 32 (over x_lo, y, z).
Axes of the slice: x: 4 (x_hi: 2, x_lo: 2; x = x_hi * 2 + x_lo), y: 4, z: 4, core: 2. Of those that a mesh axis runs over, the one named last changes fastest.
Arguments:
- acts: bfloat16 [4, 8192, 4096], P('section', 'seq'), may hold values from -6 to 6
- norm_gain: float32 [4, 4096], P('section'), may hold values from 0.1 to 1.9
- w_query: bfloat16 [4, 4096, 2048], P('section'), may hold values from -0.1875 to 0.1875
- section_key_weights: bfloat16 [4, 4096, 512], P('section', 'seq'), may hold values from -0.1875 to 0.1875
- section_value_weights: bfloat16 [4, 4096, 512], P('section', 'seq'), may hold values from -0.09375 to 0.09375
- w_out: bfloat16 [4, 2048, 4096], P('section', None, 'seq'), may hold values from -0.125 to 0.125
Outputs:
- layer_out: bfloat16 [4, 8192, 4096], P('section', 'seq')
All inputs are finite; a program needn't handle non-finite values.
Results may differ from a plain program's by a relative error of at most 0.012.
Values may be sent and summed in bfloat16 or wider, within the bound.
No kernel may reach another device: no remote copies, remote signals or barrier semaphores. Data moves between devices by JAX's collectives and lax.ppermute only.
A program may use at most 192 MiB of HBM per device.

v0:
```python
import math

import jax
import jax.numpy as jnp
from jax import lax
from jax.sharding import PartitionSpec as P

QUERY_HEAD_TOTAL = 16
KEY_VALUE_HEADS = 4
HEAD_SIZE = 128


norm_epsilon = 1e-05
rope_base = 500000.0


def shifted(x, axis, by):
    count = lax.axis_size(axis)
    return lax.ppermute(x, axis, [(i, (i + by) % count) for i in range(count)])


def rotary_tables(positions, head_width):
    freqs = rope_base ** (-2.0 * jnp.arange(head_width // 2, dtype=jnp.float32) / head_width)
    angles = positions.astype(jnp.float32)[:, None] * freqs[None, :]
    return (jnp.cos(angles)[:, None, :], jnp.sin(angles)[:, None, :])


def apply_rotary(values, cosine_table, sine_table):
    half_width = values.shape[-1] // 2
    first = values[..., :half_width]
    second = values[..., half_width:]
    return jnp.concatenate(
        [first * cosine_table - second * sine_table, second * cosine_table + first * sine_table],
        axis=-1,
    )


def body(acts, norm_gain, w_query, section_key_weights, section_value_weights, w_out):
    tokens = acts[0]
    token_rows = tokens.shape[0]
    half_rows = token_rows // 2
    seq_count = lax.axis_size("seq")
    per_device = 2 * QUERY_HEAD_TOTAL // seq_count
    group_width = QUERY_HEAD_TOTAL // KEY_VALUE_HEADS
    floats = tokens.astype(jnp.float32)
    normalized_input = (
        floats
        * lax.rsqrt(jnp.mean(floats * floats, axis=-1, keepdims=True) + norm_epsilon)
        * norm_gain[0]
    ).astype(jnp.bfloat16)
    positions = lax.axis_index("seq") * token_rows + jnp.arange(token_rows, dtype=jnp.int32)
    cosine_table, sine_table = rotary_tables(positions, HEAD_SIZE)
    query = apply_rotary(
        jnp.dot(normalized_input, w_query[0], preferred_element_type=jnp.float32).reshape(
            token_rows, QUERY_HEAD_TOTAL, HEAD_SIZE
        ),
        cosine_table,
        sine_table,
    ).astype(jnp.bfloat16)
    summed_keys = jnp.dot(
        normalized_input,
        lax.all_gather(section_key_weights[0], "seq", axis=0, tiled=True),
        preferred_element_type=jnp.float32,
    )
    summed_values = jnp.dot(
        normalized_input,
        lax.all_gather(section_value_weights[0], "seq", axis=0, tiled=True),
        preferred_element_type=jnp.float32,
    )
    local_keys = apply_rotary(
        summed_keys.reshape(token_rows, KEY_VALUE_HEADS, HEAD_SIZE), cosine_table, sine_table
    ).astype(jnp.bfloat16)
    local_values = summed_values.astype(jnp.bfloat16).reshape(
        token_rows, KEY_VALUE_HEADS, HEAD_SIZE
    )
    query_mine = lax.all_to_all(
        query.reshape(half_rows, 2 * QUERY_HEAD_TOTAL, HEAD_SIZE),
        "seq",
        split_axis=1,
        concat_axis=0,
        tiled=True,
    )
    key_all, value_all = (
        lax.all_gather(local_keys, "seq", axis=0, tiled=True),
        lax.all_gather(local_values, "seq", axis=0, tiled=True),
    )
    head_numbers = (
        lax.axis_index("seq") * per_device + jnp.arange(per_device, dtype=jnp.int32)
    ) % QUERY_HEAD_TOTAL
    selector = (
        head_numbers[:, None] // group_width
        == jnp.arange(KEY_VALUE_HEADS, dtype=jnp.int32)[None, :]
    ).astype(jnp.bfloat16)
    key_rows = jnp.einsum(
        "skd,gk->sgd", key_all, selector, preferred_element_type=jnp.float32
    ).astype(jnp.bfloat16)
    value_rows = jnp.einsum(
        "skd,gk->sgd", value_all, selector, preferred_element_type=jnp.float32
    ).astype(jnp.bfloat16)
    query_count = query_mine.shape[0]
    row_block = math.gcd(query_count, 512)
    score_scale = HEAD_SIZE ** (-0.5)

    def attend(query_block):
        scores = (
            jnp.einsum("qgd,kgd->gqk", query_block, key_rows, preferred_element_type=jnp.float32)
            * score_scale
        )
        exp_scores = jnp.exp(scores)
        softmax_out = (exp_scores / jnp.sum(exp_scores, axis=-1, keepdims=True)).astype(
            jnp.bfloat16
        )
        return jnp.einsum(
            "gqk,kgd->qgd", softmax_out, value_rows, preferred_element_type=jnp.float32
        ).astype(jnp.bfloat16)

    blocks = query_mine.reshape(query_count // row_block, row_block, per_device, HEAD_SIZE)
    attended = lax.map(attend, blocks).reshape(query_count, per_device, HEAD_SIZE)
    merged = lax.all_to_all(attended, "seq", split_axis=0, concat_axis=1, tiled=True).reshape(
        token_rows, QUERY_HEAD_TOTAL * HEAD_SIZE
    )
    branch = jnp.dot(
        merged,
        lax.all_gather(w_out[0], "seq", axis=1, tiled=True),
        preferred_element_type=jnp.float32,
    ).astype(jnp.bfloat16)
    updated = (floats + branch.astype(jnp.float32)).astype(jnp.bfloat16)
    return shifted(updated, "section", 1)[None]


def solution(mesh):
    return jax.shard_map(
        body,
        mesh=mesh,
        in_specs=(
            P("section", "seq", None),
            P("section", None),
            P("section", None, None),
            P("section", "seq", None),
            P("section", "seq", None),
            P("section", None, "seq"),
        ),
        out_specs=P("section", "seq", None),
        check_vma=False,
    )
```

profile of v0, /device:TPU:3, one launch (start us, length us, event | category | flops | bytes accessed | tf_op | source)
XLA Modules:
  0.0 982.3 jit_solution(18342737807461734660)
XLA Ops:
  6.5 0.7 all-gather.13.cloned.1.call-update
  7.3 0.7 all-gather.15.cloned.1.call-update
  8.1 2.1 fusion.36
  10.5 137.7 %all-gather.13.cloned.1.call-done = bf16[1,4096,512]{2,1,0:T(8,128)(2,1)} async-done(((bf16[1,128,512]{2,1,0:T(8,128)(2,1)}), bf16[1,4096,512]{2,1,0:T(8,128)(2,1)}) %all-gather.13.cloned.1.call-update) | async-done | bytes 4194320 | tf_op jit(solution)/shard_map/all_gather | solution.py:62
  148.2 6.6 copy.33
  154.8 3.6 fusion.52
  158.5 0.7 pad_maximum_fusion.1
  159.3 148.0 %all-gather.15.cloned.1.call-done = bf16[1,4096,512]{2,1,0:T(8,128)(2,1)} async-done(((bf16[1,128,512]{2,1,0:T(8,128)(2,1)}), bf16[1,4096,512]{2,1,0:T(8,128)(2,1)}) %all-gather.15.cloned.1.call-update) | async-done | bytes 4194320 | tf_op jit(solution)/shard_map/all_gather | solution.py:67
  307.2 3.5 fusion.47
  310.7 0.8 reshape.163
  312.1 20.8 %copy.39 = bf16[2048,4096]{1,0:T(8,128)(2,1)} copy(bf16[2048,4096]{0,1:T(8,128)(2,1)} %bitcast.132) | data formatting | bytes 33554432 | tf_op jit(solution)/shard_map/dot_general | solution.py:54
  332.9 8.3 fusion.54
  341.5 1.0 copy.30
  342.5 1.0 copy.31
  344.0 1.4 copy.32
  345.4 8.2 all-to-all-start
  353.7 135.9 %all-gather.9.cloned.1.call-done = bf16[8192,4,128]{0,2,1:T(8,128)(2,1)} async-done(((bf16[256,4,128]{0,2,1:T(8,128)(2,1)}), bf16[8192,4,128]{0,2,1:T(8,128)(2,1)}) %all-gather.9.cloned.1.call-update) | async-done | bytes 8388624 | tf_op jit(solution)/shard_map/all_gather | solution.py:84
  489.6 13.7 %copy.37 = bf16[8192,4,128]{2,1,0:T(4,128)(2,1)} copy(bf16[8192,4,128]{0,2,1:T(8,128)(2,1)} %all-gather.9.cloned.1.call-done) | data formatting | bytes 16777216 | tf_op jit(solution)/shard_map/all_gather | solution.py:84
  503.3 156.8 %all-gather.11.cloned.1.call-done = bf16[8192,4,128]{2,1,0:T(4,128)(2,1)} async-done(((bf16[256,4,128]{2,1,0:T(4,128)(2,1)}), bf16[8192,4,128]{2,1,0:T(4,128)(2,1)}) %all-gather.11.cloned.1.call-update) | async-done | bytes 8388624 | tf_op jit(solution)/shard_map/all_gather | solution.py:85
  660.1 7.4 fusion.20
  667.6 4.7 fusion.57
  672.3 1.9 convert_bitcast_fusion.1
  674.1 59.1 %while.10 = (s32[]{:T(128)}, bf16[8,512,1,128]{3,1,2,0:T(8,128)(2,1)}, bf16[8,512,1,128]{3,1,2,0:T(8,128)(2,1)S(1)}, bf16[8192,1,128]{2,0,1:T(8,128)(2,1)S(1)}, bf16[8192,1,128]{2,0,1:T(8,128)(2,1)}, /*index=5*/s32[]{:T(128)}) while((s32[]{:T(128)}, bf16[8,512,1,128]{3,1,2,0:T(8,128)(2,1)}, bf16[8,512,1,128]{3,1,2,0:T(8,128)(2,1)S(1)}, ...), condition=%wide.region_3.4_spmd, body=%wide.region_1.3_spmd.sunk | while | flops 2168520192 | bytes 46404196 | solution.py:118
  674.1 2.8 fusion.73
  677.0 4.5 fusion.74
  681.5 2.8 fusion.73
  684.3 4.5 fusion.74
  688.9 2.8 fusion.73
  691.7 4.5 fusion.74
  696.3 2.8 fusion.73
  699.1 4.5 fusion.74
  703.7 2.8 fusion.73
  706.5 4.5 fusion.74
  711.1 2.8 fusion.73
  713.9 4.5 fusion.74
  718.5 2.8 fusion.73
  721.3 4.5 fusion.74
  725.8 2.8 fusion.73
  728.7 4.5 fusion.74
  733.7 2.7 reduce.2
  736.7 19.4 %all_to_all.30 = bf16[32,2,8192]{2,1,0:T(2,128)(2,1)S(1)} all-to-all(bf16[32,2,8192]{2,1,0:T(2,128)(2,1)S(1)} %reshape.177), channel_id=1, replica_groups=mesh['section'=4,'seq'=32] {'seq'}, dimensions={0} | all-to-all | bytes 2097152 | tf_op jit(solution)/shard_map/all_to_all | solution.py:119
  756.1 1.0 reshape.178
  758.0 1.3 reshape.165
  759.3 158.9 %all-gather.17.cloned.1.call-done = bf16[1,2048,4096]{2,1,0:T(8,128)(2,1)} async-done(((bf16[1,2048,128]{2,1,0:T(8,128)(2,1)}), bf16[1,2048,4096]{2,1,0:T(8,128)(2,1)}) %all-gather.17.cloned.1.call-update) | async-done | bytes 16777232 | tf_op jit(solution)/shard_map/all_gather | solution.py:124
  918.2 10.6 %fusion.33 = bf16[256,4096]{1,0:T(8,128)(2,1)S(1)} fusion(bf16[256,2048]{1,0:T(8,128)(2,1)} %reshape.165, bf16[1,2048,4096]{2,1,0:T(8,128)(2,1)} %all-gather.17.cloned.1.call-done, bf16[1,256,4096]{2,1,0:T(8,128)(2,1)S(1)} %copy-done.2), kind=kOutput, calls=%fused_computation.25 | convolution fusion | flops 4300210176 | bytes 22020096 | tf_op jit(solution)/shard_map/dot_general | solution.py:122
  928.8 22.7 %collective-permute-start = (bf16[256,4096]{1,0:T(8,128)(2,1)S(1)}, bf16[256,4096]{1,0:T(8,128)(2,1)S(1)}, u32[]{:S(2)}, u32[]{:S(2)}) collective-permute-start(bf16[256,4096]{1,0:T(8,128)(2,1)S(1)} %fusion.33), channel_id=1, source_target_pairs={{0,32},{32,64},{64,96},{96,0},{1,33},{33,65},{65,97},{97,1},{2,34}... | collective-permute-start | bytes 6291464 | tf_op jit(solution)/shard_map/ppermute | solution.py:19
  951.5 23.0 %collective-permute-done = bf16[256,4096]{1,0:T(8,128)(2,1)S(1)} collective-permute-done((bf16[256,4096]{1,0:T(8,128)(2,1)S(1)}, bf16[256,4096]{1,0:T(8,128)(2,1)S(1)}, u32[]{:S(2)}, u32[]{:S(2)}) %collective-permute-start) | collective-permute-done | bytes 2097184 | tf_op jit(solution)/shard_map/ppermute | solution.py:19
  974.5 1.3 copy.52
  (45 shorter events, 3.7 us)
Async XLA Ops:
  6.5 141.7 %all-gather.13.cloned.1.call-start = ((), (), s32[]{:S(2)}) async-start(), calls=%async_computation.4 | async-start | bytes 4325376 | tf_op jit(solution)/shard_map/all_gather | solution.py:62
  7.3 300.0 %all-gather.15.cloned.1.call-start = ((), (), s32[]{:S(2)}) async-start(), calls=%async_computation.5 | async-start | bytes 4325376 | tf_op jit(solution)/shard_map/all_gather | solution.py:67
  8.0 481.6 %all-gather.9.cloned.1.call-start = ((), (), s32[]{:S(2)}) async-start(), calls=%async_computation.2 | async-start | bytes 8650752 | tf_op jit(solution)/shard_map/all_gather | solution.py:84
  148.2 6.6 copy-start.1
  148.2 6.6 copy-start.4
  159.2 500.9 %all-gather.11.cloned.1.call-start = ((), (), s32[]{:S(2)}) async-start(), calls=%async_computation.3 | async-start | bytes 8650752 | tf_op jit(solution)/shard_map/all_gather | solution.py:85
  311.5 606.7 %all-gather.17.cloned.1.call-start = ((), (), s32[]{:S(2)}) async-start(), calls=%async_computation.6 | async-start | bytes 17301504 | tf_op jit(solution)/shard_map/all_gather | solution.py:124
  345.4 328.7 %all-to-all-start = ((bf16[128,32,128]{2,0,1:T(8,128)(2,1)}), bf16[128,32,128]{2,0,1:T(8,128)(2,1)S(1)}, u32[]{:S(2)}, u32[]{:S(2)}) async-start(bf16[128,32,128]{2,0,1:T(8,128)(2,1)} %copy.32), calls=%async_computation | async-start | bytes 2097152 | tf_op jit(solution)/shard_map/all_to_all | solution.py:76
  660.1 7.5 copy-start
  674.1 2.8 copy-start.3
  681.5 2.8 copy-start.3
  688.9 2.8 copy-start.3
  696.3 2.8 copy-start.3
  703.7 2.8 copy-start.3
  711.1 2.8 copy-start.3
  718.4 2.8 copy-start.3
  725.8 2.8 copy-start.3
  757.3 160.9 %copy-start.2 = (bf16[1,256,4096]{2,1,0:T(8,128)(2,1)S(1)}, bf16[1,256,4096]{2,1,0:T(8,128)(2,1)}, u32[]{:S(2)}) copy-start(bf16[1,256,4096]{2,1,0:T(8,128)(2,1)} %param.8) | copy-start | bytes 6291460
  928.8 45.7 %collective-permute-start = (bf16[256,4096]{1,0:T(8,128)(2,1)S(1)}, bf16[256,4096]{1,0:T(8,128)(2,1)S(1)}, u32[]{:S(2)}, u32[]{:S(2)}) collective-permute-start(bf16[256,4096]{1,0:T(8,128)(2,1)S(1)} %fusion.33), channel_id=1, source_target_pairs={{0,32},{32,64},{64,96},{96,0},{1,33},{33,65},{65,97},{97,1},{2,34}... | collective-permute-start | bytes 6291464 | tf_op jit(solution)/shard_map/ppermute | solution.py:19
Sparse Core Ops, SparseCore 0:
  9.0 139.1 all-gather.12
  149.8 157.3 all-gather.14
  308.8 180.7 all-gather.8
  491.1 168.9 all-gather.10
  661.5 256.6 all-gather.16
where the time goes:
time: 986 us; the launch traced here: 982 us
  waiting for transfers between devices  762 us (77%)
  matrix products  97 us (10%)
  local copies, waits for them, and re-layouts  50.5 us (5%)
  starting transfers between devices  31 us (3%)
  blocking collectives  19.4 us (2%)
  between operations  13.4 us (1%)
    all_gather x1, waiting for transfers between devices, body(): lax.all_gather(w_out[0], 'seq', axis=1, tiled=True)  159 us
    all_gather x1, waiting for transfers between devices, body(): lax.all_gather(local_values, 'seq', axis=0, tiled=True)  157 us
    all_gather x1, waiting for transfers between devices, body(): lax.all_gather(section_value_weights[0], 'seq', axis=0, tiled=True)  148 us
    all_gather x1, waiting for transfers between devices, body(): lax.all_gather(section_key_weights[0], 'seq', axis=0, tiled=True)  138 us
    all_gather x1, waiting for transfers between devices, body(): lax.all_gather(local_keys, 'seq', axis=0, tiled=True)  136 us
    dot_general x8, matrix products, attend(): jnp.einsum('gqk,kgd->qgd', softmax_out, value_rows, preferred_element_typ...  36.3 us
    ppermute x1, waiting for transfers between devices, shifted(): return lax.ppermute(x, axis, [(i, (i + by) % count) for i in range(count)])  23 us
    ppermute x1, starting transfers between devices, shifted(): return lax.ppermute(x, axis, [(i, (i + by) % count) for i in range(count)])  22.7 us
  transfers between devices with their start and end apart: 7, of which 6 were waited for; matrix products, arithmetic and copies ran while one was open for 15% of the time, Pallas kernels for 0%

commit v1 on v0

v1 whole, which is shorter than its diff:
```python
import functools
import math

import jax
import jax.numpy as jnp
from jax import lax
from jax.experimental import pallas as pl
from jax.experimental.pallas import tpu as pltpu
from jax.sharding import PartitionSpec as P

HEAD = 128
EPS = 1e-05
ROPE_BASE = 500000.0
SEQ = 32
BF = jnp.bfloat16
F32 = jnp.float32
VMEM = pl.BlockSpec(memory_space=pltpu.VMEM)
SMEM = pl.BlockSpec(memory_space=pltpu.SMEM)
Q_FOLD = math.log2(math.e) / math.sqrt(HEAD)


def send(x, move):
    pairs = []
    for s in range(4):
        for d in range(SEQ):
            xh, core, xl, y, z = move(s // 2, s % 2, d // 16, d // 4 % 4, d % 4)
            pairs.append((s * SEQ + d, (xh * 2 + core) * SEQ + xl * 16 + y % 4 * 4 + z % 4))
    return lax.ppermute(x, ("section", "seq"), pairs)


def along_y(x, k):
    return send(x, lambda xh, c, b, y, z: (xh, c, b, y + k, z))


def along_z(x, k):
    return send(x, lambda xh, c, b, y, z: (xh, c, b, y, z + k))


def swap_core(x):
    return send(x, lambda xh, c, b, y, z: (xh, 1 - c, b, y, z))


def params(**kw):
    return pltpu.CompilerParams(vmem_limit_bytes=60 * 1024 * 1024, **kw)


def cost(flops, nbytes, transcendentals=0):
    return pl.CostEstimate(flops=flops, bytes_accessed=nbytes, transcendentals=transcendentals)


def query_kernel(place, x_ref, w_ref, c_ref, s_ref, o_ref):
    u = jnp.dot(x_ref[...], w_ref[0], preferred_element_type=F32)
    for h in range(4):
        v = u[:, h * HEAD : (h + 1) * HEAD]
        o_ref[0, :, h * HEAD : (h + 1) * HEAD] = (
            (v * c_ref[...] + pltpu.roll(v, 64, 1) * s_ref[...]) * Q_FOLD
        ).astype(BF)


def queries(place, x, w, c, s):
    return pl.pallas_call(
        query_kernel,
        grid_spec=pltpu.PrefetchScalarGridSpec(
            num_scalar_prefetch=1,
            grid=(4,),
            in_specs=[
                pl.BlockSpec((256, 4096), lambda k, p: (0, 0)),
                pl.BlockSpec((1, 4096, 512), lambda k, p: (0, 0, lax.rem(p[3] + k, 4))),
                pl.BlockSpec((256, HEAD), lambda k, p: (0, 0)),
                pl.BlockSpec((256, HEAD), lambda k, p: (0, 0)),
            ],
            out_specs=pl.BlockSpec((1, 256, 512), lambda k, p: (k, 0, 0)),
        ),
        out_shape=jax.ShapeDtypeStruct((4, 256, 512), BF),
        compiler_params=params(),
        cost_estimate=cost(2 * 256 * 4096 * 2048, 20 << 20),
        name="queries",
    )(place, x, w, c, s)


def kv_kernel(place, own, oth, c_ref, s_ref, *rest):
    first, second = rest[0:4], rest[4:8]
    o_ref, acc = rest[8:]
    core, y, z = place[0], place[2], place[3]

    def columns(ref, blocks):
        return jnp.concatenate(
            [ref[:, pl.ds(pl.multiple_of(b * 128, 128), 128)] for b in blocks], axis=1
        )

    for which in range(8):
        if which < 4:
            w = first[which]
            blocks = [core * 16 + lax.rem(y + 4 - m, 4) * 4 + lax.rem(z + 4 - which, 4) for m in range(4)]
        else:
            w = second[which - 4]
            blocks = [
                (1 - core) * 16 + lax.rem(y + 8 - which, 4) * 4 + lax.rem(z + 4 - j, 4)
                for j in range(4)
            ]
        for t, ref in enumerate((own, oth)):
            part = jnp.dot(columns(ref, blocks), w[...], preferred_element_type=F32)
            if which == 0:
                acc[t] = part
            else:
                acc[t] += part
    for t in range(2):
        row = pl.multiple_of(lax.select(t == 0, core, 1 - core) * 256, 256)
        for k in range(4):
            v = acc[t, :, pl.ds(pl.multiple_of(lax.rem(z + k, 4) * HEAD, HEAD), HEAD)]
            o_ref[k, pl.ds(row, 256), :] = (v * c_ref[t] + pltpu.roll(v, 64, 1) * s_ref[t]).astype(BF)


def keys_or_values(place, own, oth, c, s, first, second):
    return pl.pallas_call(
        kv_kernel,
        in_specs=[SMEM] + [VMEM] * 12,
        out_specs=VMEM,
        out_shape=jax.ShapeDtypeStruct((4, 512, HEAD), BF),
        scratch_shapes=[pltpu.VMEM((2, 256, 512), F32)],
        compiler_params=params(),
        cost_estimate=cost(2 * 512 * 4096 * 512, 9 << 20),
        name="keys_or_values",
    )(place, own, oth, c, s, *first, *second)


def attend_kernel(place, *refs):
    q = refs[0:4]
    mine, other = refs[4:8], refs[8:12]
    o_ref, kv, vv = refs[12:]
    core = place[0]
    vv[:, :, HEAD:] = jnp.ones((4, 2048, HEAD), BF)
    for m in range(4):
        kv[m, core] = mine[m][...]
        kv[m, 1 - core] = other[m][...]
        vv[m, :, :HEAD] = kv[m, 1]

    for k in range(4):
        for h in range(4):
            qb = q[k][:, h * HEAD : (h + 1) * HEAD]

            def step(m, carry):
                top, acc = carry
                sc = lax.dot_general(qb, kv[m, 0], (((1,), (1,)), ((), ())), preferred_element_type=F32)
                new = jnp.maximum(top, jnp.max(sc, axis=1, keepdims=True))
                p = jnp.exp2(sc - new).astype(BF)
                acc = acc * jnp.exp2(top - new) + jnp.dot(p, vv[m], preferred_element_type=F32)
                return new, acc

            top = jnp.full((256, 1), -1e30, F32)
            _, acc = lax.fori_loop(0, 4, step, (top, jnp.zeros((256, 256), F32)))
            o_ref[k, :, h * HEAD : (h + 1) * HEAD] = (acc[:, :HEAD] / acc[:, HEAD:]).astype(BF)


def attend(place, q, mine, other):
    return pl.pallas_call(
        attend_kernel,
        in_specs=[SMEM] + [VMEM] * 12,
        out_specs=VMEM,
        out_shape=jax.ShapeDtypeStruct((4, 256, 512), BF),
        scratch_shapes=[pltpu.VMEM((4, 2, 2048, HEAD), BF), pltpu.VMEM((4, 2048, 2 * HEAD), BF)],
        compiler_params=params(),
        cost_estimate=cost(4 * 4096 * 8192 * 256, 6 << 20, 4096 * 8192),
        name="attend",
    )(place, *q, *mine, *other)


def project_kernel(place, *refs):
    att, own, oth, o_ref = refs[0:4], refs[4], refs[5], refs[6]
    z = place[3]
    for half, w in enumerate((own, oth)):
        for j in range(4):
            row = pl.multiple_of(lax.rem(z + 4 - j, 4) * 512, 512)
            wj = jnp.concatenate([w[m, pl.ds(row, 512), :] for m in range(4)], axis=1)
            for k in range(4):
                part = jnp.dot(att[j][(k - j) % 4], wj, preferred_element_type=F32)
                acc = refs[7]
                if j == 0:
                    acc[k] = part
                elif j < 3:
                    acc[k] += part
                else:
                    o_ref[k, :, half * 512 : (half + 1) * 512] = (acc[k] + part).astype(BF)


def project(place, att, own, oth):
    return pl.pallas_call(
        project_kernel,
        in_specs=[SMEM] + [VMEM] * 6,
        out_specs=VMEM,
        out_shape=jax.ShapeDtypeStruct((4, 256, 1024), BF),
        scratch_shapes=[pltpu.VMEM((4, 256, 512), F32)],
        compiler_params=params(),
        cost_estimate=cost(2 * 1024 * 2048 * 1024, 10 << 20),
        name="project",
    )(place, *att, own, oth)


def residual_kernel(place, acts, *refs):
    branch, o_ref = refs[0:4], refs[4]
    xl, y, z = place[1], place[2], place[3]
    for k in range(4):
        for half in range(2):
            b = xl if half == 0 else 1 - xl
            for m in range(4):
                block = b * 16 + lax.rem(y + 4 - m, 4) * 4 + lax.rem(z + k, 4)
                at = pl.ds(pl.multiple_of(block * 128, 128), 128)
                i = (half * 4 + m) * 128
                o_ref[:, at] = (acts[:, at].astype(F32) + branch[k][:, i : i + 128].astype(F32)).astype(BF)


def residual(place, acts, branch):
    return pl.pallas_call(
        residual_kernel,
        in_specs=[SMEM] + [VMEM] * 5,
        out_specs=VMEM,
        out_shape=jax.ShapeDtypeStruct((256, 4096), BF),
        compiler_params=params(),
        cost_estimate=cost(256 * 4096, 6 << 20),
        name="residual",
    )(place, acts, *branch)


def tables(seq_index):
    freqs = ROPE_BASE ** (-2.0 * jnp.arange(HEAD // 2, dtype=F32) / HEAD)
    positions = seq_index * 256 + jnp.arange(256, dtype=jnp.int32)
    angles = positions.astype(F32)[:, None] * freqs[None, :]
    cosine, sine = jnp.cos(angles), jnp.sin(angles)
    return jnp.concatenate([cosine, cosine], 1), jnp.concatenate([-sine, sine], 1)


def turn(xh, c, b, y, z):
    return xh, b, c, y, z


def body(acts, norm_gain, w_query, w_key, w_value, w_out):
    section, seq = lax.axis_index("section"), lax.axis_index("seq")
    core, xl, y, z = section % 2, seq // 16, seq // 4 % 4, seq % 4
    place = jnp.stack([core, xl, y, z]).astype(jnp.int32)
    tokens = acts[0]
    low = xl == 0
    half0 = send(jnp.where(low, w_key[0], w_value[0]), turn)
    half1 = send(
        jnp.where(low, w_value[0], w_key[0]), lambda xh, c, b, y, z: (xh, 1 - b, c, y, z)
    )
    floats = tokens.astype(F32)
    normed = (
        floats * lax.rsqrt(jnp.mean(floats * floats, axis=-1, keepdims=True) + EPS) * norm_gain[0]
    ).astype(BF)
    own = send(normed, turn)
    other = swap_core(own)
    first = jnp.concatenate([half0] + [along_y(half0, m) for m in (1, 2, 3)], 0)
    second = jnp.concatenate([half1] + [along_z(half1, j) for j in (1, 2, 3)], 0)
    firsts = [first] + [along_z(first, j) for j in (1, 2, 3)]
    seconds = [second] + [along_y(second, m) for m in (1, 2, 3)]

    cos_n, sin_n = tables(seq)
    q = queries(place, normed, w_query, cos_n, sin_n)
    q = [
        send(q[k], lambda xh, c, b, y, z, k=k: (xh, b, c, y, z + k)) for k in range(4)
    ]

    is_key = core == 0
    rope = [tables(b * 16 + y * 4 + z) for b in (core, 1 - core)]
    cos_k = jnp.where(is_key, jnp.stack([t[0] for t in rope]), 1.0)
    sin_k = jnp.where(is_key, jnp.stack([t[1] for t in rope]), 0.0)
    kv = keys_or_values(place, own, other, cos_k, sin_k, firsts, seconds)
    kv = jnp.concatenate([kv[0]] + [along_z(kv[k], k) for k in (1, 2, 3)], 0)
    mine = [kv] + [along_y(kv, m) for m in (1, 2, 3)]
    theirs = [swap_core(a) for a in mine]
    att = attend(place, q, mine, theirs)

    w_own = send(w_out[0], turn)
    w_own = jnp.stack([w_own] + [along_y(w_own, m) for m in (1, 2, 3)])
    w_other = swap_core(w_own)
    atts = [att] + [along_z(att, j) for j in (1, 2, 3)]
    branch = project(place, atts, w_own, w_other)

    def home(k):
        def move(xh, c, b, y, z):
            s = (2 * xh + b + 1) % 4
            return s // 2, s % 2, c, y, z - k

        return move

    branch = [send(branch[k], home(k)) for k in range(4)]

    def onward(xh, c, b, y, z):
        s = (2 * xh + c + 1) % 4
        return s // 2, s % 2, b, y, z

    return residual(place, send(tokens, onward), branch)[None]


def solution(mesh):
    return jax.shard_map(
        body,
        mesh=mesh,
        in_specs=(
            P("section", "seq", None),
            P("section", None),
            P("section", None, None),
            P("section", "seq", None),
            P("section", "seq", None),
            P("section", None, "seq"),
        ),
        out_specs=P("section", "seq", None),
        check_vma=False,
    )
```

time: 986 us -> 386 us (0.39)
  waiting for transfers between devices: 762 us -> 144 us
  Pallas kernels: 0 us -> 126 us
  matrix products: 97 us -> 0 us
  starting transfers between devices: 31 us -> 88.3 us
  local copies, waits for them, and re-layouts: 50.5 us -> 6.8 us
  blocking collectives: 19.4 us -> 0 us
  between operations: 13.4 us -> 0.83 us
    all_gather x5 -> x0, waiting for transfers between devices: 737 us -> none  [the longest x1 159 us: body(): lax.all_gather(w_out[0], 'seq', axis=1, tiled=True)]
    pallas_call x0 -> x5, Pallas kernels: none -> 126 us  [the longest x1 94.5 us: attend(): pl.pallas_call(attend_kernel, in_specs=[SMEM] + [VMEM] * 12, out_specs=VM...]
    ppermute x1 -> x43, waiting for transfers between devices: 23 us -> 144 us  [send(): return lax.ppermute(x, ('section', 'seq'), pairs)]
    dot_general x21 -> x0, matrix products: 89.5 us -> none  [the longest x8 36.3 us: attend(): jnp.einsum('gqk,kgd->qgd', softmax_out, value_rows, preferred_element_typ...]
    ppermute x1 -> x43, starting transfers between devices: 22.7 us -> 88.3 us  [send(): return lax.ppermute(x, ('section', 'seq'), pairs)]
    dot_general x2 -> x0, local copies, waits for them, and re-layouts: 27.4 us -> none  [the longest x1 20.8 us: body(): jnp.dot(normalized_input, w_query[0], preferred_element_type=jnp.float32)]
    all_to_all x1 -> x0, blocking collectives: 19.4 us -> none  [body(): lax.all_to_all(attended, 'seq', split_axis=0, concat_axis=1, tiled=True)]
    all_gather x1 -> x0, local copies, waits for them, and re-layouts: 13.7 us -> none  [body(): lax.all_gather(local_keys, 'seq', axis=0, tiled=True)]
  transfers between devices with their start and end apart: 7 -> 43, of which waited for: 6 -> 20; matrix products, arithmetic and copies ran while one was open for 15% -> 3% of each run, Pallas kernels for 0% -> 32%
where the time goes in v1:
time: 386 us; the launch traced here: 378 us
  waiting for transfers between devices  144 us (37%)
  Pallas kernels  126 us (33%)
  starting transfers between devices  88.3 us (23%)
  other arithmetic  11.7 us (3%)
  local copies, waits for them, and re-layouts  6.8 us (2%)
    ppermute x43, waiting for transfers between devices, send(): return lax.ppermute(x, ('section', 'seq'), pairs)  144 us
    pallas_call x1, Pallas kernels, attend(): pl.pallas_call(attend_kernel, in_specs=[SMEM] + [VMEM] * 12, out_specs=VM...  94.5 us
    ppermute x43, starting transfers between devices, send(): return lax.ppermute(x, ('section', 'seq'), pairs)  88.3 us
    pallas_call x1, Pallas kernels, queries(): pl.pallas_call(query_kernel, grid_spec=pltpu.PrefetchScalarGridSpec(num_s...  11 us
    pallas_call x1, Pallas kernels, project(): pl.pallas_call(project_kernel, in_specs=[SMEM] + [VMEM] * 6, out_specs=VM...  9.34 us
  transfers between devices with their start and end apart: 43, of which 20 were waited for; matrix products, arithmetic and copies ran while one was open for 3% of the time, Pallas kernels for 32%

profile of v1, /device:TPU:3, one launch (start us, length us, event | category | flops | bytes accessed | tf_op | source)
XLA Modules:
  0.0 378.0 jit_solution(18370002589242831920)
XLA Ops:
  0.0 2.2 fusion
  2.3 1.4 fusion.2.x_ref
  3.7 2.0 collective-permute-start.5
  6.5 2.2 collective-permute-start.7
  8.6 2.2 collective-permute-start.14
  10.8 5.4 %collective-permute-start.34 = (bf16[2048,128]{1,0:T(8,128)(2,1)}, bf16[2048,128]{1,0:T(8,128)(2,1)}, u32[]{:S(2)}, u32[]{:S(2)}) collective-permute-start(bf16[2048,128]{1,0:T(8,128)(2,1)} %bitcast.20), channel_id=1, source_target_pairs={{0,0},{1,1},{2,2},{3,3},{4,4},{5,5},{6,6},{7,7},{8,8},{9,9},{10,10... | collective-permute-start | bytes 1572872 | tf_op jit(solution)/shard_map/ppermute | solution.py:28
  16.3 15.6 %collective-permute-start.6 = (bf16[256,4096]{1,0:T(8,128)(2,1)}, bf16[256,4096]{1,0:T(8,128)(2,1)}, u32[]{:S(2)}, u32[]{:S(2)}) collective-permute-start(bf16[256,4096]{1,0:T(8,128)(2,1)} %collective-permute-done.5.own), channel_id=1, source_target_pairs={{0,32},{1,33},{2,34},{3,35},{4,36},{5,37},{6,38},{7,39},{8,40},{9,... | collective-permute-start | bytes 6291464 | tf_op jit(solution)/shard_map/ppermute | solution.py:28
  31.8 1.4 fusion.4
  33.6 1.4 collective-permute-start.8
  35.7 2.6 collective-permute-start.9
  40.4 1.6 collective-permute-start.15
  42.0 2.2 collective-permute-done.9
  44.2 3.6 collective-permute-start.16
  51.7 2.2 collective-permute-start.17
  54.0 11.7 %collective-permute-done.17 = bf16[128,512]{1,0:T(8,128)(2,1)S(1)} collective-permute-done((bf16[128,512]{1,0:T(8,128)(2,1)}, bf16[128,512]{1,0:T(8,128)(2,1)S(1)}, u32[]{:S(2)}, u32[]{:S(2)}) %collective-permute-start.17) | collective-permute-done | bytes 131104 | tf_op jit(solution)/shard_map/ppermute | solution.py:28
  65.7 3.4 collective-permute-start.13
  70.1 4.1 %collective-permute-done.12.rest_2_ = bf16[512,512]{1,0:T(8,128)(2,1)S(1)} collective-permute-done((bf16[512,512]{1,0:T(8,128)(2,1)S(1)}, bf16[512,512]{1,0:T(8,128)(2,1)S(1)}, u32[]{:S(2)}, u32[]{:S(2)}) %collective-permute-start.12) | collective-permute-done | bytes 524320 | tf_op jit(solution)/shard_map/ppermute | solution.py:28
  76.5 11.0 %queries.1 = bf16[4,256,512]{2,1,0:T(8,128)(2,1)} custom-call(s32[4]{0:T(128)} %pad_add_fusion.place, bf16[256,4096]{1,0:T(8,128)(2,1)} %copy-done, bf16[1,4096,2048]{2,1,0:T(8,128)(2,1)} %w_ref.1, f32[256,128]{1,0:T(8,128)} %get-tuple-element.34.c_ref, f32[256,128]{1,0:T(8,128)} %get-tuple-element.35.s_ref), custom_call_target="tpu_custom_call" | custom-call | flops 4294967296 | bytes 20971520 | tf_op jit(solution)/shard_map/queries/pallas_call | solution.py:61
  88.4 5.5 %collective-permute-done.18.rest_5_ = bf16[512,512]{1,0:T(8,128)(2,1)} collective-permute-done((bf16[512,512]{1,0:T(8,128)(2,1)S(1)}, bf16[512,512]{1,0:T(8,128)(2,1)}, u32[]{:S(2)}, u32[]{:S(2)}) %collective-permute-start.18) | collective-permute-done | bytes 524320 | tf_op jit(solution)/shard_map/ppermute | solution.py:28
  93.9 1.3 collective-permute-done.20.rest_7_
  95.1 7.1 %keys_or_values.1 = bf16[4,512,128]{2,1,0:T(8,128)(2,1)} custom-call(s32[4]{0:T(128)} %pad_add_fusion.place, bf16[256,4096]{1,0:T(8,128)(2,1)} %collective-permute-done.5.own, bf16[256,4096]{1,0:T(8,128)(2,1)} %collective-permute-done.6.oth, f32[2,256,128]{2,1,0:T(8,128)} %maximum_select_fusion.c_ref, f32[2,256,128]{2,1,0:T(8,128)} %maximum_select_fusion.1.s_ref, ...), custom_call_target="tpu_custom_call" | custom-call | flops 2147483648 | bytes 9437184 | tf_op jit(solution)/shard_map/keys_or_values/pallas_call | solution.py:115
  104.7 1.5 collective-permute-start.23
  106.9 3.0 collective-permute-done.21
  111.6 5.3 %collective-permute-start.24 = (bf16[2048,128]{1,0:T(8,128)(2,1)S(1)}, bf16[2048,128]{1,0:T(8,128)(2,1)S(1)}, u32[]{:S(2)}, u32[]{:S(2)}) collective-permute-start(bf16[2048,128]{1,0:T(8,128)(2,1)S(1)} %pad_maximum_fusion.1.refs_4_), channel_id=1, source_target_pairs={{0,4},{1,5},{2,6},{3,7},{4,8},{5,9},{6,10},{7,11},{8,12},{9,13},{1... | collective-permute-start | bytes 1572872 | tf_op jit(solution)/shard_map/ppermute | solution.py:28
  116.9 8.1 %collective-permute-done.2.refs_1_ = bf16[256,512]{1,0:T(8,128)(2,1)S(1)} collective-permute-done((bf16[256,512]{1,0:T(8,128)(2,1)S(1)}, bf16[256,512]{1,0:T(8,128)(2,1)S(1)}, u32[]{:S(2)}, u32[]{:S(2)}) %collective-permute-start.2) | collective-permute-done | bytes 262176 | tf_op jit(solution)/shard_map/ppermute | solution.py:28
  126.1 5.0 %collective-permute-start.26 = (bf16[2048,128]{1,0:T(8,128)(2,1)S(1)}, bf16[2048,128]{1,0:T(8,128)(2,1)S(1)}, u32[]{:S(2)}, u32[]{:S(2)}) collective-permute-start(bf16[2048,128]{1,0:T(8,128)(2,1)S(1)} %pad_maximum_fusion.1.refs_4_), channel_id=1, source_target_pairs={{0,12},{1,13},{2,14},{3,15},{4,0},{5,1},{6,2},{7,3},{8,4},{9,5},{1... | collective-permute-start | bytes 1572872 | tf_op jit(solution)/shard_map/ppermute | solution.py:28
  131.9 10.6 %collective-permute-done.24.refs_5_ = bf16[2048,128]{1,0:T(8,128)(2,1)S(1)} collective-permute-done((bf16[2048,128]{1,0:T(8,128)(2,1)S(1)}, bf16[2048,128]{1,0:T(8,128)(2,1)S(1)}, u32[]{:S(2)}, u32[]{:S(2)}) %collective-permute-start.24) | collective-permute-done | bytes 524320 | tf_op jit(solution)/shard_map/ppermute | solution.py:28
  144.0 5.4 %collective-permute-start.29 = (bf16[2048,128]{1,0:T(8,128)(2,1)S(1)}, bf16[2048,128]{1,0:T(8,128)(2,1)S(1)}, u32[]{:S(2)}, u32[]{:S(2)}) collective-permute-start(bf16[2048,128]{1,0:T(8,128)(2,1)S(1)} %collective-permute-done.25.refs_6_), channel_id=1, source_target_pairs={{0,32},{1,33},{2,34},{3,35},{4,36},{5,37},{6,38},{7,39},{8,40},{9,... | collective-permute-start | bytes 1572872 | tf_op jit(solution)/shard_map/ppermute | solution.py:28
  149.4 6.0 %collective-permute-done.26.refs_7_ = bf16[2048,128]{1,0:T(8,128)(2,1)S(1)} collective-permute-done((bf16[2048,128]{1,0:T(8,128)(2,1)S(1)}, bf16[2048,128]{1,0:T(8,128)(2,1)S(1)}, u32[]{:S(2)}, u32[]{:S(2)}) %collective-permute-start.26) | collective-permute-done | bytes 524320 | tf_op jit(solution)/shard_map/ppermute | solution.py:28
  155.4 7.5 %collective-permute-done.37 = bf16[2048,128]{1,0:T(8,128)(2,1)S(1)} collective-permute-done((bf16[2048,128]{1,0:T(8,128)(2,1)}, bf16[2048,128]{1,0:T(8,128)(2,1)S(1)}, u32[]{:S(2)}, u32[]{:S(2)}) %collective-permute-start.37) | collective-permute-done | bytes 524320 | tf_op jit(solution)/shard_map/ppermute | solution.py:28
  162.9 2.8 collective-permute-start.4
  165.7 2.6 pad_maximum_fusion.refs_4_
  168.4 3.5 collective-permute-done.4.refs_3_
  173.7 94.5 %attend.1.refs_0_ = bf16[4,256,512]{2,1,0:T(8,128)(2,1)} custom-call(s32[4]{0:T(128)} %pad_add_fusion.place, bf16[256,512]{1,0:T(8,128)(2,1)} %copy-done.22, bf16[256,512]{1,0:T(8,128)(2,1)} %copy-done.23, bf16[256,512]{1,0:T(8,128)(2,1)} %collective-permute-done.3.refs_2_, bf16[256,512]{1,0:T(8,128)(2,1)} %copy-done.24, bf16[2048,128]{1,0:T(8,128)(2,1)} %copy-done.12, ...), custom_call_target="tpu_custom_call" | custom-call | flops 34359738368 | bytes 6291456 | tf_op jit(solution)/shard_map/attend/pallas_call | solution.py:156
  268.2 1.4 collective-permute-start.31
  269.6 2.9 collective-permute-start.32
  272.5 2.7 collective-permute-start
  275.3 19.5 %collective-permute-done.31.refs_1_ = bf16[4,256,512]{2,1,0:T(8,128)(2,1)S(1)} collective-permute-done((bf16[4,256,512]{2,1,0:T(8,128)(2,1)}, bf16[4,256,512]{2,1,0:T(8,128)(2,1)S(1)}, u32[]{:S(2)}, u32[]{:S(2)}) %collective-permute-start.31) | collective-permute-done | bytes 1048608 | tf_op jit(solution)/shard_map/ppermute | solution.py:28
  294.7 23.4 %collective-permute-done.32.refs_2_ = bf16[4,256,512]{2,1,0:T(8,128)(2,1)} collective-permute-done((bf16[4,256,512]{2,1,0:T(8,128)(2,1)}, bf16[4,256,512]{2,1,0:T(8,128)(2,1)}, u32[]{:S(2)}, u32[]{:S(2)}) %collective-permute-start.32) | collective-permute-done | bytes 1048608 | tf_op jit(solution)/shard_map/ppermute | solution.py:28
  318.2 9.3 %project.1 = bf16[4,256,1024]{2,1,0:T(8,128)(2,1)} custom-call(s32[4]{0:T(128)} %pad_add_fusion.place, bf16[4,256,512]{2,1,0:T(8,128)(2,1)} %attend.1.refs_0_, bf16[4,256,512]{2,1,0:T(8,128)(2,1)} %copy-done.15, bf16[4,256,512]{2,1,0:T(8,128)(2,1)} %collective-permute-done.32.refs_2_, bf16[4,256,512]{2,1,0:T(8,128)(2,1)} %collective-permute-done.33.refs_3_, ...), custom_call_target="tpu_custom_call" | custom-call | flops 4294967296 | bytes 10485760 | tf_op jit(solution)/shard_map/project/pallas_call | solution.py:187
  327.5 1.7 slice_bitcast_fusion
  329.2 3.1 collective-permute-start.39
  332.3 4.2 %collective-permute-start.40 = (bf16[256,1024]{1,0:T(8,128)(2,1)S(1)}, bf16[256,1024]{1,0:T(8,128)(2,1)S(1)}, u32[]{:S(2)}, u32[]{:S(2)}) collective-permute-start(bf16[256,1024]{1,0:T(8,128)(2,1)S(1)} %get-tuple-element.7), channel_id=1, source_target_pairs={{0,35},{1,32},{2,33},{3,34},{4,39},{5,36},{6,37},{7,38},{8,43},{9,... | collective-permute-start | bytes 1572872 | tf_op jit(solution)/shard_map/ppermute | solution.py:28
  337.2 1.9 collective-permute-done.39.refs_0_
  339.1 12.6 %collective-permute-done.40.refs_1_ = bf16[256,1024]{1,0:T(8,128)(2,1)S(1)} collective-permute-done((bf16[256,1024]{1,0:T(8,128)(2,1)S(1)}, bf16[256,1024]{1,0:T(8,128)(2,1)S(1)}, u32[]{:S(2)}, u32[]{:S(2)}) %collective-permute-start.40) | collective-permute-done | bytes 524320 | tf_op jit(solution)/shard_map/ppermute | solution.py:28
  351.7 11.3 %collective-permute-done.41.refs_2_ = bf16[256,1024]{1,0:T(8,128)(2,1)S(1)} collective-permute-done((bf16[256,1024]{1,0:T(8,128)(2,1)S(1)}, bf16[256,1024]{1,0:T(8,128)(2,1)S(1)}, u32[]{:S(2)}, u32[]{:S(2)}) %collective-permute-start.41) | collective-permute-done | bytes 524320 | tf_op jit(solution)/shard_map/ppermute | solution.py:28
  362.9 10.3 %collective-permute-done.42.refs_3_ = bf16[256,1024]{1,0:T(8,128)(2,1)} collective-permute-done((bf16[256,1024]{1,0:T(8,128)(2,1)S(1)}, bf16[256,1024]{1,0:T(8,128)(2,1)}, u32[]{:S(2)}, u32[]{:S(2)}) %collective-permute-start.42) | collective-permute-done | bytes 524320 | tf_op jit(solution)/shard_map/ppermute | solution.py:28
  373.2 4.3 %residual.1 = bf16[256,4096]{1,0:T(8,128)(2,1)} custom-call(s32[4]{0:T(128)} %pad_add_fusion.place, bf16[256,4096]{1,0:T(8,128)(2,1)} %collective-permute-done.acts, bf16[256,1024]{1,0:T(8,128)(2,1)} %copy-done.9, bf16[256,1024]{1,0:T(8,128)(2,1)} %copy-done.10, bf16[256,1024]{1,0:T(8,128)(2,1)} %copy-done.11, bf16[256,1024]{1,0:T(8,128)(2,1)} %collective-permute-done.42.refs_3_), custom_call_target="tpu_custom_call" | custom-call | flops 1048576 | bytes 6291456 | tf_op jit(solution)/shard_map/residual/pallas_call | solution.py:213
  (121 shorter events, 22.7 us)
Async XLA Ops:
  3.7 12.6 %collective-permute-start.5 = (bf16[256,4096]{1,0:T(8,128)(2,1)S(1)}, bf16[256,4096]{1,0:T(8,128)(2,1)}, u32[]{:S(2)}, u32[]{:S(2)}) collective-permute-start(bf16[256,4096]{1,0:T(8,128)(2,1)S(1)} %fusion.2.x_ref), channel_id=1, source_target_pairs={{0,0},{1,1},{2,2},{3,3},{4,4},{5,5},{6,6},{7,7},{8,8},{9,9},{10,10... | collective-permute-start | bytes 6291464 | tf_op jit(solution)/shard_map/ppermute | solution.py:28
  6.5 27.1 %collective-permute-start.7 = (bf16[128,512]{1,0:T(8,128)(2,1)}, bf16[128,512]{1,0:T(8,128)(2,1)}, u32[]{:S(2)}, u32[]{:S(2)}) collective-permute-start(bf16[128,512]{1,0:T(8,128)(2,1)} %get-tuple-element.18), channel_id=1, source_target_pairs={{0,0},{1,1},{2,2},{3,3},{4,4},{5,5},{6,6},{7,7},{8,8},{9,9},{10,10... | collective-permute-start | bytes 393224 | tf_op jit(solution)/shard_map/ppermute | solution.py:28
  8.6 30.6 %collective-permute-start.14 = (bf16[128,512]{1,0:T(8,128)(2,1)}, bf16[128,512]{1,0:T(8,128)(2,1)}, u32[]{:S(2)}, u32[]{:S(2)}) collective-permute-start(bf16[128,512]{1,0:T(8,128)(2,1)} %get-tuple-element.17), channel_id=1, source_target_pairs={{0,32},{1,33},{2,34},{3,35},{4,36},{5,37},{6,38},{7,39},{8,40},{9,... | collective-permute-start | bytes 393224 | tf_op jit(solution)/shard_map/ppermute | solution.py:28
  10.8 58.4 %collective-permute-start.34 = (bf16[2048,128]{1,0:T(8,128)(2,1)}, bf16[2048,128]{1,0:T(8,128)(2,1)}, u32[]{:S(2)}, u32[]{:S(2)}) collective-permute-start(bf16[2048,128]{1,0:T(8,128)(2,1)} %bitcast.20), channel_id=1, source_target_pairs={{0,0},{1,1},{2,2},{3,3},{4,4},{5,5},{6,6},{7,7},{8,8},{9,9},{10,10... | collective-permute-start | bytes 1572872 | tf_op jit(solution)/shard_map/ppermute | solution.py:28
  16.3 78.9 %collective-permute-start.6 = (bf16[256,4096]{1,0:T(8,128)(2,1)}, bf16[256,4096]{1,0:T(8,128)(2,1)}, u32[]{:S(2)}, u32[]{:S(2)}) collective-permute-start(bf16[256,4096]{1,0:T(8,128)(2,1)} %collective-permute-done.5.own), channel_id=1, source_target_pairs={{0,32},{1,33},{2,34},{3,35},{4,36},{5,37},{6,38},{7,39},{8,40},{9,... | collective-permute-start | bytes 6291464 | tf_op jit(solution)/shard_map/ppermute | solution.py:28
  33.6 6.8 %collective-permute-start.8 = (bf16[128,512]{1,0:T(8,128)(2,1)}, bf16[128,512]{1,0:T(8,128)(2,1)S(1)}, u32[]{:S(2)}, u32[]{:S(2)}) collective-permute-start(bf16[128,512]{1,0:T(8,128)(2,1)} %collective-permute-done.7), channel_id=1, source_target_pairs={{0,4},{1,5},{2,6},{3,7},{4,8},{5,9},{6,10},{7,11},{8,12},{9,13},{1... | collective-permute-start | bytes 393224 | tf_op jit(solution)/shard_map/ppermute | solution.py:28
  35.7 8.6 %collective-permute-start.9 = (bf16[128,512]{1,0:T(8,128)(2,1)}, bf16[128,512]{1,0:T(8,128)(2,1)S(1)}, u32[]{:S(2)}, u32[]{:S(2)}) collective-permute-start(bf16[128,512]{1,0:T(8,128)(2,1)} %collective-permute-done.7), channel_id=1, source_target_pairs={{0,8},{1,9},{2,10},{3,11},{4,12},{5,13},{6,14},{7,15},{8,0},{9,1},... | collective-permute-start | bytes 393224 | tf_op jit(solution)/shard_map/ppermute | solution.py:28
  39.2 8.6 %collective-permute-start.10 = (bf16[128,512]{1,0:T(8,128)(2,1)}, bf16[128,512]{1,0:T(8,128)(2,1)S(1)}, u32[]{:S(2)}, u32[]{:S(2)}) collective-permute-start(bf16[128,512]{1,0:T(8,128)(2,1)} %collective-permute-done.7), channel_id=1, source_target_pairs={{0,12},{1,13},{2,14},{3,15},{4,0},{5,1},{6,2},{7,3},{8,4},{9,5},{1... | collective-permute-start | bytes 393224 | tf_op jit(solution)/shard_map/ppermute | solution.py:28
  40.4 8.3 %collective-permute-start.15 = (bf16[128,512]{1,0:T(8,128)(2,1)}, bf16[128,512]{1,0:T(8,128)(2,1)S(1)}, u32[]{:S(2)}, u32[]{:S(2)}) collective-permute-start(bf16[128,512]{1,0:T(8,128)(2,1)} %collective-permute-done.14), channel_id=1, source_target_pairs={{0,1},{1,2},{2,3},{3,0},{4,5},{5,6},{6,7},{7,4},{8,9},{9,10},{10,1... | collective-permute-start | bytes 393224 | tf_op jit(solution)/shard_map/ppermute | solution.py:28
  44.2 7.5 %collective-permute-start.16 = (bf16[128,512]{1,0:T(8,128)(2,1)}, bf16[128,512]{1,0:T(8,128)(2,1)S(1)}, u32[]{:S(2)}, u32[]{:S(2)}) collective-permute-start(bf16[128,512]{1,0:T(8,128)(2,1)} %collective-permute-done.14), channel_id=1, source_target_pairs={{0,2},{1,3},{2,0},{3,1},{4,6},{5,7},{6,4},{7,5},{8,10},{9,11},{10,... | collective-permute-start | bytes 393224 | tf_op jit(solution)/shard_map/ppermute | solution.py:28
  47.9 39.7 %copy-start.4 = (bf16[512,512]{1,0:T(8,128)(2,1)}, bf16[512,512]{1,0:T(8,128)(2,1)S(1)}, u32[]{:S(2)}) copy-start(bf16[512,512]{1,0:T(8,128)(2,1)S(1)} %constant_dynamic-update-slice_fusion.rest_0_) | copy-start | bytes 1572868
  47.9 21.5 %collective-permute-start.11 = (bf16[512,512]{1,0:T(8,128)(2,1)S(1)}, bf16[512,512]{1,0:T(8,128)(2,1)S(1)}, u32[]{:S(2)}, u32[]{:S(2)}) collective-permute-start(bf16[512,512]{1,0:T(8,128)(2,1)S(1)} %constant_dynamic-update-slice_fusion.rest_0_), channel_id=1, source_target_pairs={{0,1},{1,2},{2,3},{3,0},{4,5},{5,6},{6,7},{7,4},{8,9},{9,10},{10,1... | collective-permute-start | bytes 1572872 | tf_op jit(solution)/shard_map/ppermute | solution.py:28
  48.7 25.5 %collective-permute-start.12 = (bf16[512,512]{1,0:T(8,128)(2,1)S(1)}, bf16[512,512]{1,0:T(8,128)(2,1)S(1)}, u32[]{:S(2)}, u32[]{:S(2)}) collective-permute-start(bf16[512,512]{1,0:T(8,128)(2,1)S(1)} %constant_dynamic-update-slice_fusion.rest_0_), channel_id=1, source_target_pairs={{0,2},{1,3},{2,0},{3,1},{4,6},{5,7},{6,4},{7,5},{8,10},{9,11},{10,... | collective-permute-start | bytes 1572872 | tf_op jit(solution)/shard_map/ppermute | solution.py:28
  51.7 14.0 %collective-permute-start.17 = (bf16[128,512]{1,0:T(8,128)(2,1)}, bf16[128,512]{1,0:T(8,128)(2,1)S(1)}, u32[]{:S(2)}, u32[]{:S(2)}) collective-permute-start(bf16[128,512]{1,0:T(8,128)(2,1)} %collective-permute-done.14), channel_id=1, source_target_pairs={{0,3},{1,0},{2,1},{3,2},{4,7},{5,4},{6,5},{7,6},{8,11},{9,8},{10,9... | collective-permute-start | bytes 393224 | tf_op jit(solution)/shard_map/ppermute | solution.py:28
  65.7 21.8 %collective-permute-start.13 = (bf16[512,512]{1,0:T(8,128)(2,1)S(1)}, bf16[512,512]{1,0:T(8,128)(2,1)S(1)}, u32[]{:S(2)}, u32[]{:S(2)}) collective-permute-start(bf16[512,512]{1,0:T(8,128)(2,1)S(1)} %constant_dynamic-update-slice_fusion.rest_0_), channel_id=1, source_target_pairs={{0,3},{1,0},{2,1},{3,2},{4,7},{5,4},{6,5},{7,6},{8,11},{9,8},{10,9... | collective-permute-start | bytes 1572872 | tf_op jit(solution)/shard_map/ppermute | solution.py:28
  69.2 24.6 %collective-permute-start.18 = (bf16[512,512]{1,0:T(8,128)(2,1)S(1)}, bf16[512,512]{1,0:T(8,128)(2,1)}, u32[]{:S(2)}, u32[]{:S(2)}) collective-permute-start(bf16[512,512]{1,0:T(8,128)(2,1)S(1)} %constant_dynamic-update-slice_fusion.4.rest_4_), channel_id=1, source_target_pairs={{0,4},{1,5},{2,6},{3,7},{4,8},{5,9},{6,10},{7,11},{8,12},{9,13},{1... | collective-permute-start | bytes 1572872 | tf_op jit(solution)/shard_map/ppermute | solution.py:28
  69.4 24.4 %collective-permute-start.19 = (bf16[512,512]{1,0:T(8,128)(2,1)S(1)}, bf16[512,512]{1,0:T(8,128)(2,1)}, u32[]{:S(2)}, u32[]{:S(2)}) collective-permute-start(bf16[512,512]{1,0:T(8,128)(2,1)S(1)} %constant_dynamic-update-slice_fusion.4.rest_4_), channel_id=1, source_target_pairs={{0,8},{1,9},{2,10},{3,11},{4,12},{5,13},{6,14},{7,15},{8,0},{9,1},... | collective-permute-start | bytes 1572872 | tf_op jit(solution)/shard_map/ppermute | solution.py:28
  74.2 20.9 %collective-permute-start.20 = (bf16[512,512]{1,0:T(8,128)(2,1)S(1)}, bf16[512,512]{1,0:T(8,128)(2,1)}, u32[]{:S(2)}, u32[]{:S(2)}) collective-permute-start(bf16[512,512]{1,0:T(8,128)(2,1)S(1)} %constant_dynamic-update-slice_fusion.4.rest_4_), channel_id=1, source_target_pairs={{0,12},{1,13},{2,14},{3,15},{4,0},{5,1},{6,2},{7,3},{8,4},{9,5},{1... | collective-permute-start | bytes 1572872 | tf_op jit(solution)/shard_map/ppermute | solution.py:28
  87.6 43.5 %collective-permute-start.35 = (bf16[2048,128]{1,0:T(8,128)(2,1)}, bf16[2048,128]{1,0:T(8,128)(2,1)S(1)}, u32[]{:S(2)}, u32[]{:S(2)}) collective-permute-start(bf16[2048,128]{1,0:T(8,128)(2,1)} %collective-permute-done.34), channel_id=1, source_target_pairs={{0,4},{1,5},{2,6},{3,7},{4,8},{5,9},{6,10},{7,11},{8,12},{9,13},{1... | collective-permute-start | bytes 1572872 | tf_op jit(solution)/shard_map/ppermute | solution.py:28
  103.4 6.5 %collective-permute-start.21 = (bf16[512,128]{1,0:T(8,128)(2,1)S(1)}, bf16[512,128]{1,0:T(8,128)(2,1)S(1)}, u32[]{:S(2)}, u32[]{:S(2)}) collective-permute-start(bf16[512,128]{1,0:T(8,128)(2,1)S(1)} %get-tuple-element.16), channel_id=1, source_target_pairs={{0,1},{1,2},{2,3},{3,0},{4,5},{5,6},{6,7},{7,4},{8,9},{9,10},{10,1... | collective-permute-start | bytes 393224 | tf_op jit(solution)/shard_map/ppermute | solution.py:28
  103.5 6.4 %collective-permute-start.22 = (bf16[512,128]{1,0:T(8,128)(2,1)S(1)}, bf16[512,128]{1,0:T(8,128)(2,1)S(1)}, u32[]{:S(2)}, u32[]{:S(2)}) collective-permute-start(bf16[512,128]{1,0:T(8,128)(2,1)S(1)} %get-tuple-element.15), channel_id=1, source_target_pairs={{0,2},{1,3},{2,0},{3,1},{4,6},{5,7},{6,4},{7,5},{8,10},{9,11},{10,... | collective-permute-start | bytes 393224 | tf_op jit(solution)/shard_map/ppermute | solution.py:28
  104.7 6.1 %collective-permute-start.23 = (bf16[512,128]{1,0:T(8,128)(2,1)S(1)}, bf16[512,128]{1,0:T(8,128)(2,1)S(1)}, u32[]{:S(2)}, u32[]{:S(2)}) collective-permute-start(bf16[512,128]{1,0:T(8,128)(2,1)S(1)} %get-tuple-element.14), channel_id=1, source_target_pairs={{0,3},{1,0},{2,1},{3,2},{4,7},{5,4},{6,5},{7,6},{8,11},{9,8},{10,9... | collective-permute-start | bytes 393224 | tf_op jit(solution)/shard_map/ppermute | solution.py:28
  106.2 5.4 %collective-permute-start.1 = (bf16[256,512]{1,0:T(8,128)(2,1)S(1)}, bf16[256,512]{1,0:T(8,128)(2,1)S(1)}, u32[]{:S(2)}, u32[]{:S(2)}) collective-permute-start(bf16[256,512]{1,0:T(8,128)(2,1)S(1)} %get-tuple-element.12), channel_id=1, source_target_pairs={{0,0},{1,1},{2,2},{3,3},{4,4},{5,5},{6,6},{7,7},{8,8},{9,9},{10,10... | collective-permute-start | bytes 786440 | tf_op jit(solution)/shard_map/ppermute | solution.py:28
  109.9 15.2 %collective-permute-start.2 = (bf16[256,512]{1,0:T(8,128)(2,1)S(1)}, bf16[256,512]{1,0:T(8,128)(2,1)S(1)}, u32[]{:S(2)}, u32[]{:S(2)}) collective-permute-start(bf16[256,512]{1,0:T(8,128)(2,1)S(1)} %get-tuple-element.11), channel_id=1, source_target_pairs={{0,1},{1,2},{2,3},{3,0},{4,5},{5,6},{6,7},{7,4},{8,9},{9,10},{10,1... | collective-permute-start | bytes 786440 | tf_op jit(solution)/shard_map/ppermute | solution.py:28
  109.9 16.2 %collective-permute-start.3 = (bf16[256,512]{1,0:T(8,128)(2,1)S(1)}, bf16[256,512]{1,0:T(8,128)(2,1)}, u32[]{:S(2)}, u32[]{:S(2)}) collective-permute-start(bf16[256,512]{1,0:T(8,128)(2,1)S(1)} %get-tuple-element.10), channel_id=1, source_target_pairs={{0,2},{1,3},{2,0},{3,1},{4,6},{5,7},{6,4},{7,5},{8,10},{9,11},{10,... | collective-permute-start | bytes 786440 | tf_op jit(solution)/shard_map/ppermute | solution.py:28
  110.8 20.4 %collective-permute-start.36 = (bf16[2048,128]{1,0:T(8,128)(2,1)}, bf16[2048,128]{1,0:T(8,128)(2,1)S(1)}, u32[]{:S(2)}, u32[]{:S(2)}) collective-permute-start(bf16[2048,128]{1,0:T(8,128)(2,1)} %collective-permute-done.34), channel_id=1, source_target_pairs={{0,8},{1,9},{2,10},{3,11},{4,12},{5,13},{6,14},{7,15},{8,0},{9,1},... | collective-permute-start | bytes 1572872 | tf_op jit(solution)/shard_map/ppermute | solution.py:28
  111.6 56.8 %copy-start.12 = (bf16[2048,128]{1,0:T(8,128)(2,1)}, bf16[2048,128]{1,0:T(8,128)(2,1)S(1)}, u32[]{:S(2)}) copy-start(bf16[2048,128]{1,0:T(8,128)(2,1)S(1)} %pad_maximum_fusion.1.refs_4_) | copy-start | bytes 1572868
  111.6 56.7 %copy-start.22 = (bf16[256,512]{1,0:T(8,128)(2,1)}, bf16[256,512]{1,0:T(8,128)(2,1)S(1)}, u32[]{:S(2)}) copy-start(bf16[256,512]{1,0:T(8,128)(2,1)S(1)} %collective-permute-done.1.refs_0_) | copy-start | bytes 786436
  111.6 30.8 %collective-permute-start.24 = (bf16[2048,128]{1,0:T(8,128)(2,1)S(1)}, bf16[2048,128]{1,0:T(8,128)(2,1)S(1)}, u32[]{:S(2)}, u32[]{:S(2)}) collective-permute-start(bf16[2048,128]{1,0:T(8,128)(2,1)S(1)} %pad_maximum_fusion.1.refs_4_), channel_id=1, source_target_pairs={{0,4},{1,5},{2,6},{3,7},{4,8},{5,9},{6,10},{7,11},{8,12},{9,13},{1... | collective-permute-start | bytes 1572872 | tf_op jit(solution)/shard_map/ppermute | solution.py:28
  125.0 40.7 %copy-start.23 = (bf16[256,512]{1,0:T(8,128)(2,1)}, bf16[256,512]{1,0:T(8,128)(2,1)S(1)}, u32[]{:S(2)}) copy-start(bf16[256,512]{1,0:T(8,128)(2,1)S(1)} %collective-permute-done.2.refs_1_) | copy-start | bytes 786436
  125.0 19.0 %collective-permute-start.25 = (bf16[2048,128]{1,0:T(8,128)(2,1)S(1)}, bf16[2048,128]{1,0:T(8,128)(2,1)S(1)}, u32[]{:S(2)}, u32[]{:S(2)}) collective-permute-start(bf16[2048,128]{1,0:T(8,128)(2,1)S(1)} %pad_maximum_fusion.1.refs_4_), channel_id=1, source_target_pairs={{0,8},{1,9},{2,10},{3,11},{4,12},{5,13},{6,14},{7,15},{8,0},{9,1},... | collective-permute-start | bytes 1572872 | tf_op jit(solution)/shard_map/ppermute | solution.py:28
  126.1 29.2 %collective-permute-start.26 = (bf16[2048,128]{1,0:T(8,128)(2,1)S(1)}, bf16[2048,128]{1,0:T(8,128)(2,1)S(1)}, u32[]{:S(2)}, u32[]{:S(2)}) collective-permute-start(bf16[2048,128]{1,0:T(8,128)(2,1)S(1)} %pad_maximum_fusion.1.refs_4_), channel_id=1, source_target_pairs={{0,12},{1,13},{2,14},{3,15},{4,0},{5,1},{6,2},{7,3},{8,4},{9,5},{1... | collective-permute-start | bytes 1572872 | tf_op jit(solution)/shard_map/ppermute | solution.py:28
  131.1 31.8 %collective-permute-start.37 = (bf16[2048,128]{1,0:T(8,128)(2,1)}, bf16[2048,128]{1,0:T(8,128)(2,1)S(1)}, u32[]{:S(2)}, u32[]{:S(2)}) collective-permute-start(bf16[2048,128]{1,0:T(8,128)(2,1)} %collective-permute-done.34), channel_id=1, source_target_pairs={{0,12},{1,13},{2,14},{3,15},{4,0},{5,1},{6,2},{7,3},{8,4},{9,5},{1... | collective-permute-start | bytes 1572872 | tf_op jit(solution)/shard_map/ppermute | solution.py:28
  131.2 40.7 %collective-permute-start.27 = (bf16[2048,128]{1,0:T(8,128)(2,1)S(1)}, bf16[2048,128]{1,0:T(8,128)(2,1)S(1)}, u32[]{:S(2)}, u32[]{:S(2)}) collective-permute-start(bf16[2048,128]{1,0:T(8,128)(2,1)S(1)} %pad_maximum_fusion.1.refs_4_), channel_id=1, source_target_pairs={{0,32},{1,33},{2,34},{3,35},{4,36},{5,37},{6,38},{7,39},{8,40},{9,... | collective-permute-start | bytes 1572872 | tf_op jit(solution)/shard_map/ppermute | solution.py:28
  142.4 29.4 %collective-permute-start.28 = (bf16[2048,128]{1,0:T(8,128)(2,1)S(1)}, bf16[2048,128]{1,0:T(8,128)(2,1)S(1)}, u32[]{:S(2)}, u32[]{:S(2)}) collective-permute-start(bf16[2048,128]{1,0:T(8,128)(2,1)S(1)} %collective-permute-done.24.refs_5_), channel_id=1, source_target_pairs={{0,32},{1,33},{2,34},{3,35},{4,36},{5,37},{6,38},{7,39},{8,40},{9,... | collective-permute-start | bytes 1572872 | tf_op jit(solution)/shard_map/ppermute | solution.py:28
  144.0 27.9 %collective-permute-start.29 = (bf16[2048,128]{1,0:T(8,128)(2,1)S(1)}, bf16[2048,128]{1,0:T(8,128)(2,1)S(1)}, u32[]{:S(2)}, u32[]{:S(2)}) collective-permute-start(bf16[2048,128]{1,0:T(8,128)(2,1)S(1)} %collective-permute-done.25.refs_6_), channel_id=1, source_target_pairs={{0,32},{1,33},{2,34},{3,35},{4,36},{5,37},{6,38},{7,39},{8,40},{9,... | collective-permute-start | bytes 1572872 | tf_op jit(solution)/shard_map/ppermute | solution.py:28
  155.4 18.4 %collective-permute-start.30 = (bf16[2048,128]{1,0:T(8,128)(2,1)S(1)}, bf16[2048,128]{1,0:T(8,128)(2,1)}, u32[]{:S(2)}, u32[]{:S(2)}) collective-permute-start(bf16[2048,128]{1,0:T(8,128)(2,1)S(1)} %collective-permute-done.26.refs_7_), channel_id=1, source_target_pairs={{0,32},{1,33},{2,34},{3,35},{4,36},{5,37},{6,38},{7,39},{8,40},{9,... | collective-permute-start | bytes 1572872 | tf_op jit(solution)/shard_map/ppermute | solution.py:28
  162.9 8.9 %collective-permute-start.4 = (bf16[256,512]{1,0:T(8,128)(2,1)S(1)}, bf16[256,512]{1,0:T(8,128)(2,1)S(1)}, u32[]{:S(2)}, u32[]{:S(2)}) collective-permute-start(bf16[256,512]{1,0:T(8,128)(2,1)S(1)} %get-tuple-element.9), channel_id=1, source_target_pairs={{0,3},{1,0},{2,1},{3,2},{4,7},{5,4},{6,5},{7,6},{8,11},{9,8},{10,9... | collective-permute-start | bytes 786440 | tf_op jit(solution)/shard_map/ppermute | solution.py:28
  168.4 104.2 %copy-start.2 = (bf16[1,256,4096]{2,1,0:T(8,128)(2,1)S(1)}, bf16[1,256,4096]{2,1,0:T(8,128)(2,1)}, u32[]{:S(2)}) copy-start(bf16[1,256,4096]{2,1,0:T(8,128)(2,1)} %param.6) | copy-start | bytes 6291460
  171.8 103.4 %collective-permute-start.38 = (bf16[4,2048,128]{2,1,0:T(8,128)(2,1)}, bf16[4,2048,128]{2,1,0:T(8,128)(2,1)}, u32[]{:S(2)}, u32[]{:S(2)}) collective-permute-start(bf16[4,2048,128]{2,1,0:T(8,128)(2,1)} %pad_maximum_fusion.refs_4_), channel_id=1, source_target_pairs={{0,32},{1,33},{2,34},{3,35},{4,36},{5,37},{6,38},{7,39},{8,40},{9,... | collective-permute-start | bytes 6291464 | tf_op jit(solution)/shard_map/ppermute | solution.py:28
  268.2 26.5 %collective-permute-start.31 = (bf16[4,256,512]{2,1,0:T(8,128)(2,1)}, bf16[4,256,512]{2,1,0:T(8,128)(2,1)S(1)}, u32[]{:S(2)}, u32[]{:S(2)}) collective-permute-start(bf16[4,256,512]{2,1,0:T(8,128)(2,1)} %attend.1.refs_0_), channel_id=1, source_target_pairs={{0,1},{1,2},{2,3},{3,0},{4,5},{5,6},{6,7},{7,4},{8,9},{9,10},{10,1... | collective-permute-start | bytes 3145736 | tf_op jit(solution)/shard_map/ppermute | solution.py:28
  269.6 48.5 %collective-permute-start.32 = (bf16[4,256,512]{2,1,0:T(8,128)(2,1)}, bf16[4,256,512]{2,1,0:T(8,128)(2,1)}, u32[]{:S(2)}, u32[]{:S(2)}) collective-permute-start(bf16[4,256,512]{2,1,0:T(8,128)(2,1)} %attend.1.refs_0_), channel_id=1, source_target_pairs={{0,2},{1,3},{2,0},{3,1},{4,6},{5,7},{6,4},{7,5},{8,10},{9,11},{10,... | collective-permute-start | bytes 3145736 | tf_op jit(solution)/shard_map/ppermute | solution.py:28
  272.5 45.6 %collective-permute-start.33 = (bf16[4,256,512]{2,1,0:T(8,128)(2,1)}, bf16[4,256,512]{2,1,0:T(8,128)(2,1)}, u32[]{:S(2)}, u32[]{:S(2)}) collective-permute-start(bf16[4,256,512]{2,1,0:T(8,128)(2,1)} %attend.1.refs_0_), channel_id=1, source_target_pairs={{0,3},{1,0},{2,1},{3,2},{4,7},{5,4},{6,5},{7,6},{8,11},{9,8},{10,9... | collective-permute-start | bytes 3145736 | tf_op jit(solution)/shard_map/ppermute | solution.py:28
  272.5 64.7 %collective-permute-start = (bf16[256,4096]{1,0:T(8,128)(2,1)S(1)}, bf16[256,4096]{1,0:T(8,128)(2,1)}, u32[]{:S(2)}, u32[]{:S(2)}) collective-permute-start(bf16[256,4096]{1,0:T(8,128)(2,1)S(1)} %bitcast.50), channel_id=1, source_target_pairs={{0,32},{1,33},{2,34},{3,35},{4,36},{5,37},{6,38},{7,39},{8,40},{9,... | collective-permute-start | bytes 6291464 | tf_op jit(solution)/shard_map/ppermute | solution.py:28
  329.2 9.9 %collective-permute-start.39 = (bf16[256,1024]{1,0:T(8,128)(2,1)S(1)}, bf16[256,1024]{1,0:T(8,128)(2,1)S(1)}, u32[]{:S(2)}, u32[]{:S(2)}) collective-permute-start(bf16[256,1024]{1,0:T(8,128)(2,1)S(1)} %get-tuple-element.8), channel_id=1, source_target_pairs={{0,32},{1,33},{2,34},{3,35},{4,36},{5,37},{6,38},{7,39},{8,40},{9,... | collective-permute-start | bytes 1572872 | tf_op jit(solution)/shard_map/ppermute | solution.py:28
  332.3 19.4 %collective-permute-start.40 = (bf16[256,1024]{1,0:T(8,128)(2,1)S(1)}, bf16[256,1024]{1,0:T(8,128)(2,1)S(1)}, u32[]{:S(2)}, u32[]{:S(2)}) collective-permute-start(bf16[256,1024]{1,0:T(8,128)(2,1)S(1)} %get-tuple-element.7), channel_id=1, source_target_pairs={{0,35},{1,32},{2,33},{3,34},{4,39},{5,36},{6,37},{7,38},{8,43},{9,... | collective-permute-start | bytes 1572872 | tf_op jit(solution)/shard_map/ppermute | solution.py:28
  336.5 26.4 %collective-permute-start.41 = (bf16[256,1024]{1,0:T(8,128)(2,1)S(1)}, bf16[256,1024]{1,0:T(8,128)(2,1)S(1)}, u32[]{:S(2)}, u32[]{:S(2)}) collective-permute-start(bf16[256,1024]{1,0:T(8,128)(2,1)S(1)} %get-tuple-element.6), channel_id=1, source_target_pairs={{0,34},{1,35},{2,32},{3,33},{4,38},{5,39},{6,36},{7,37},{8,42},{9,... | collective-permute-start | bytes 1572872 | tf_op jit(solution)/shard_map/ppermute | solution.py:28
  337.2 36.0 %collective-permute-start.42 = (bf16[256,1024]{1,0:T(8,128)(2,1)S(1)}, bf16[256,1024]{1,0:T(8,128)(2,1)}, u32[]{:S(2)}, u32[]{:S(2)}) collective-permute-start(bf16[256,1024]{1,0:T(8,128)(2,1)S(1)} %get-tuple-element.5), channel_id=1, source_target_pairs={{0,33},{1,34},{2,35},{3,32},{4,37},{5,38},{6,39},{7,36},{8,41},{9,... | collective-permute-start | bytes 1572872 | tf_op jit(solution)/shard_map/ppermute | solution.py:28
  (20 other events, 279.5 us)
